TPU v7x, 128 devices: a whole 4x4x4 slice. The times are simulated.
128 devices in a mesh: ctg: 16 (over y, x), line: 8 (over z, core).
Axes of the slice: x: 4, y: 4, z: 4, core: 2. Of those that a mesh axis runs over, the one named last changes fastest.
Arguments:
- base_flow: float32 [384, 15360], P(None, ('ctg', 'line')), may hold values from -6 to 6
- lodf: bfloat16 [15360, 15360], P('line', 'ctg'), may hold values from -0.3125 to 0.3125
- dual: bfloat16 [15360, 15360], P('line', 'ctg'), may hold values from 0 to 2.5, as said below
- rating: float32 [15360], P('line'), may hold values from 0.3 to 2
- sens: bfloat16 [15360, 2048], P('line', 'ctg'), may hold values from -0.046875 to 0.046875
- fetch_rows: int32 [16, 128, 15], P('ctg'), may hold values from -1 to 119, as said below
- ctg_slot: int32 [15360], P('ctg'), may hold values from 0 to 1919, as said below
Outputs:
- cut: float32 [2048, 384], P(('ctg', 'line'))
Inputs may be any that keep to these rules, and one draw needn't show every extreme that they name: `fetch_rows`: -1 marks an empty slot; other entries are distinct columns of flow holder o's block of 120 lines; some pairs (c, o) may have no live slot, and one flow holder has all 15 slots live for every contingency holder. `ctg_slot`: the 960 contingencies of holder c take distinct slots o * 15 + j, exactly the live entries of fetch_rows[c]. `dual`: zero outside the overloaded pairs, positive on them.
All inputs are finite; a program needn't handle non-finite values.
Results may differ from a plain program's by a relative error of at most 0.0059.
Values may be sent and summed in bfloat16 or wider, within the bound.
A program may use at most 64 MiB of HBM per device.

v0:
```python
import jax
import jax.numpy as jnp
from jax import lax
from jax.sharding import PartitionSpec as P


def soft_excess(flow_sum, rating):
    return jnp.sign(flow_sum) * jnp.maximum(jnp.abs(flow_sum) - rating[None, :], 0.0)


def per_device(base_flow, lodf, dual, rating, sens, fetch_rows, ctg_slot):
    columns_total = base_flow.shape[0]
    requests = fetch_rows[0]
    asked = lax.all_to_all(requests, ("ctg", "line"), split_axis=0, concat_axis=0, tiled=True)
    live_slot = asked >= 0
    columns = jnp.where(live_slot, asked, 0)
    values = jnp.take(base_flow, columns.reshape(-1), axis=1)
    values = values.reshape(columns_total, asked.shape[0], asked.shape[1])
    replies = lax.all_to_all(
        jnp.where(live_slot[None], values, 0.0).astype(jnp.bfloat16),
        ("ctg", "line"),
        split_axis=1,
        concat_axis=1,
        tiled=True,
    )
    slot_flows = replies.reshape(columns_total, -1)
    outage_flow = jnp.take(slot_flows, ctg_slot, axis=1)
    weighted = (dual.astype(jnp.float32) * lodf.astype(jnp.float32)).astype(jnp.bfloat16)
    partial_value = lax.dot_general(
        outage_flow, weighted, (((1,), (1,)), ((), ())), preferred_element_type=jnp.float32
    )
    totals = lax.psum(partial_value, "ctg")
    excess = soft_excess(totals, rating).astype(jnp.bfloat16)
    columns = sens
    return lax.psum_scatter(
        lax.dot_general(
            columns, excess, (((0,), (1,)), ((), ())), preferred_element_type=jnp.float32
        ),
        "line",
        scatter_dimension=0,
        tiled=True,
    )


def solution(mesh):
    in_specs = (
        P(None, ("ctg", "line")),
        P("line", "ctg"),
        P("line", "ctg"),
        P("line"),
        P("line", "ctg"),
        P("ctg", None, None),
        P("ctg"),
    )
    out_specs = P(("ctg", "line"), None)
    return jax.shard_map(
        per_device, mesh=mesh, in_specs=in_specs, out_specs=out_specs, check_vma=False
    )
```

profile of v0, /device:TPU:0, one launch (start us, length us, event | category | flops | bytes accessed | tf_op | source)
XLA Modules:
  0.0 210.2 jit_solution(16124836973732095510)
XLA Ops:
  6.5 0.9 copy.22
  7.4 20.5 %all_to_all.20 = s32[128,1,15]{2,1,0:T(1,128)S(1)} all-to-all(s32[128,1,15]{2,1,0:T(1,128)S(1)} %copy.22), channel_id=1, replica_groups=mesh['ctg'=16,'line'=8] {'ctg','line'}, dimensions={0} | all-to-all | bytes 15360 | tf_op jit(solution)/shard_map/all_to_all | solution.py:14
  27.9 0.1 copy.23
  28.0 0.5 broadcast.84
  28.5 0.8 reduce.5
  29.3 0.2 all_to_all.16
  29.6 0.1 copy.24
  29.7 0.7 copy.25
  30.4 5.0 %gather_fusion = bf16[1920,384]{1,0:T(8,128)(2,1)S(1)} fusion(f32[384,120]{0,1:T(8,128)S(1)} %copy-done.1, s32[2048]{0:T(1024)S(1)} %pad_clamp_fusion), kind=kCustom, calls=%fused_computation | custom fusion | bytes 2956800 | tf_op jit(solution)/shard_map/jit(_take)/gather | solution.py:17
  35.5 0.5 gather.11
  36.0 3.1 %select_convert_fusion = bf16[384,128,15]{0,2,1:T(8,128)(2,1)} fusion(bf16[384,128,15]{0,2,1:T(8,128)(2,1)S(1)} %gather.11, pred[128,15]{1,0:T(8,128)(4,1)} %copy.25, pred[128,15]{1,0:T(8,128)(4,1)S(1)} %copy.24), kind=kLoop, calls=%fused_computation.4 | loop fusion | flops 1474560 | bytes 2952960 | tf_op jit(solution)/shard_map/convert_element_type | solution.py:20
  39.1 4.6 %all-to-all-start.1 = ((bf16[384,128,15]{0,2,1:T(8,128)(2,1)}), bf16[384,128,15]{0,2,1:T(8,128)(2,1)S(1)}, u32[]{:S(2)}, u32[]{:S(2)}) async-start(bf16[384,128,15]{0,2,1:T(8,128)(2,1)} %select_convert_fusion), calls=%async_computation.1 | async-start | bytes 3145728 | tf_op jit(solution)/shard_map/all_to_all | solution.py:19
  43.7 0.0 all-reduce.2.cloned.1.call-start
  43.8 24.8 %all-to-all-done.1 = bf16[384,128,15]{0,2,1:T(8,128)(2,1)S(1)} async-done(((bf16[384,128,15]{0,2,1:T(8,128)(2,1)}), bf16[384,128,15]{0,2,1:T(8,128)(2,1)S(1)}, u32[]{:S(2)}, u32[]{:S(2)}) %all-to-all-start.1) | async-done | bytes 1474592 | tf_op jit(solution)/shard_map/all_to_all | solution.py:19
  68.6 0.5 reshape.60
  69.1 4.1 %gather_fusion.1 = bf16[960,384]{1,0:T(8,128)(2,1)S(1)} fusion(bf16[384,1920]{0,1:T(8,128)(2,1)S(1)} %reshape.60, s32[1024]{0:T(1024)S(1)} %pad_clamp_fusion.1), kind=kCustom, calls=%fused_computation.1 | custom fusion | bytes 1478400 | tf_op jit(solution)/shard_map/jit(_take)/gather | solution.py:27
  73.2 6.7 %fusion = f32[384,1920]{1,0:T(8,128)} fusion(bf16[1920,960]{0,1:T(8,128)(2,1)} %param.8, bf16[1920,960]{0,1:T(8,128)(2,1)} %param.9, bf16[960,384]{1,0:T(8,128)(2,1)S(1)} %gather_fusion.1, pred[960]{0:T(1024)(128)(4,1)S(1)} %compare_and_fusion.1), kind=kOutput, calls=%fused_computation.3 | convolution fusion | flops 1423319040 | bytes 11060160 | tf_op jit(solution)/shard_map/dot_general | solution.py:29
  79.9 0.0 all-reduce.2.cloned.1.call-update
  79.9 0.0 reduce-scatter.4.cloned.1.call-start
  80.0 89.5 %all-reduce.2.cloned.1.call-done = f32[384,1920]{1,0:T(8,128)} async-done(((f32[384,1920]{1,0:T(8,128)}), f32[384,1920]{1,0:T(8,128)}) %all-reduce.2.cloned.1.call-update) | async-done | bytes 2949136 | tf_op jit(solution)/shard_map/psum | solution.py:32
  169.5 3.1 %fusion.2 = f32[128,384]{0,1:T(8,128)S(1)} fusion(bf16[1920,128]{1,0:T(8,128)(2,1)S(1)} %copy-done, f32[384,1920]{1,0:T(8,128)} %all-reduce.2.cloned.1.call-done, f32[1920]{0:T(1024)S(1)} %copy-done.3), kind=kOutput, calls=%fused_computation.7 | convolution fusion | flops 193167360 | bytes 3644928 | tf_op jit(solution)/shard_map/dot_general | solution.py:36
  172.5 0.8 copy.27
  173.3 0.0 reduce-scatter.4.cloned.1.call-update
  173.4 30.0 %reduce-scatter.4.cloned.1.call-done = f32[16,384]{1,0:T(8,128)} async-done(((f32[128,384]{1,0:T(8,128)}), f32[16,384]{1,0:T(8,128)}) %reduce-scatter.4.cloned.1.call-update) | async-done | bytes 24592 | tf_op jit(solution)/shard_map/reduce_scatter | solution.py:35
  (14 shorter events, 0.1 us)
Async XLA Ops:
  6.5 162.9 %copy-start = (bf16[1920,128]{1,0:T(8,128)(2,1)S(1)}, bf16[1920,128]{1,0:T(8,128)(2,1)}, u32[]{:S(2)}) copy-start(bf16[1920,128]{1,0:T(8,128)(2,1)} %param.11) | copy-start | bytes 1474564
  6.5 23.9 %copy-start.1 = (f32[384,120]{0,1:T(8,128)S(1)}, f32[384,120]{0,1:T(8,128)}, u32[]{:S(2)}) copy-start(f32[384,120]{0,1:T(8,128)} %param.7) | copy-start | bytes 552964
  36.0 7.8 %copy-start.2 = (s32[960]{0:T(1024)S(1)}, s32[960]{0:T(1024)}, u32[]{:S(2)}) copy-start(s32[960]{0:T(1024)} %param.13) | copy-start | bytes 11524
  39.1 29.5 %all-to-all-start.1 = ((bf16[384,128,15]{0,2,1:T(8,128)(2,1)}), bf16[384,128,15]{0,2,1:T(8,128)(2,1)S(1)}, u32[]{:S(2)}, u32[]{:S(2)}) async-start(bf16[384,128,15]{0,2,1:T(8,128)(2,1)} %select_convert_fusion), calls=%async_computation.1 | async-start | bytes 3145728 | tf_op jit(solution)/shard_map/all_to_all | solution.py:19
  43.7 125.8 %all-reduce.2.cloned.1.call-start = ((), (), s32[]{:S(2)}) async-start(), calls=%async_computation.3 | async-start | bytes 5898240 | tf_op jit(solution)/shard_map/psum | solution.py:32
  79.9 89.6 %copy-start.3 = (f32[1920]{0:T(1024)S(1)}, f32[1920]{0:T(1024)}, u32[]{:S(2)}) copy-start(f32[1920]{0:T(1024)} %param.10) | copy-start | bytes 23044
  79.9 123.5 %reduce-scatter.4.cloned.1.call-start = ((), (), s32[]{:S(2)}) async-start(), calls=%async_computation.4 | async-start | bytes 221184 | tf_op jit(solution)/shard_map/reduce_scatter | solution.py:35
Sparse Core Ops, SparseCore 0:
  80.1 89.3 all-reduce.1
  173.5 29.8 reduce-scatter.3
where the time goes:
time: 211 us; the launch traced here: 210 us
  waiting for transfers between devices  144 us (68%)
  blocking collectives  20.5 us (10%)
  local copies, waits for them, and re-layouts  13.5 us (6%)
  between operations  13.5 us (6%)
  matrix products  9.77 us (5%)
  starting transfers between devices  4.72 us (2%)
  other arithmetic  3.98 us (2%)
    psum x1, waiting for transfers between devices, per_device(): totals = lax.psum(partial_value, 'ctg')  89.5 us
    reduce_scatter x1, waiting for transfers between devices, per_device(): lax.psum_scatter(lax.dot_general(columns, excess, (((0,), (1,)), ((), ())...  30 us
    all_to_all x1, waiting for transfers between devices, per_device(): lax.all_to_all(jnp.where(live_slot[None], values, 0.0).astype(jnp.bfloat1...  24.8 us
    all_to_all x1, blocking collectives, per_device(): lax.all_to_all(requests, ('ctg', 'line'), split_axis=0, concat_axis=0, ti...  20.5 us
    dot_general x1, matrix products, per_device(): lax.dot_general(outage_flow, weighted, (((1,), (1,)), ((), ())), preferre...  6.72 us
    gather x2, local copies, waits for them, and re-layouts, per_device(): values = jnp.take(base_flow, columns.reshape(-1), axis=1)  5.54 us
    all_to_all x1, starting transfers between devices, per_device(): lax.all_to_all(jnp.where(live_slot[None], values, 0.0).astype(jnp.bfloat1...  4.64 us
  transfers between devices with their start and end apart: 3, of which 3 were waited for; matrix products, arithmetic and copies ran while one was open for 0% of the time, Pallas kernels for 0%

commit v1 on v0

--- a/solution.py
+++ b/solution.py
@@ -29,7 +29,7 @@
     partial_value = lax.dot_general(
         outage_flow, weighted, (((1,), (1,)), ((), ())), preferred_element_type=jnp.float32
     )
-    totals = lax.psum(partial_value, "ctg")
+    totals = jnp.sum(lax.all_gather(partial_value, "ctg"), axis=0)
     excess = soft_excess(totals, rating).astype(jnp.bfloat16)
     columns = sens
     return lax.psum_scatter(

time: 211 us -> 400 us (1.90)
  waiting for transfers between devices: 144 us -> 317 us
  other arithmetic: 3.98 us -> 20.4 us
    all_gather x0 -> x1, waiting for transfers between devices: none -> 262 us  [per_device(): totals = jnp.sum(lax.all_gather(partial_value, 'ctg'), axis=0)]
    psum x1 -> x0, waiting for transfers between devices: 89.5 us -> none  [per_device(): totals = lax.psum(partial_value, 'ctg')]
    reduce_sum x0 -> x1, other arithmetic: none -> 16.4 us  [per_device(): totals = jnp.sum(lax.all_gather(partial_value, 'ctg'), axis=0)]
where the time goes in v1:
time: 400 us
  waiting for transfers between devices  317 us (79%)
  blocking collectives  20.5 us (5%)
  other arithmetic  20.4 us (5%)
  local copies, waits for them, and re-layouts  14.4 us (4%)
  between operations  13.5 us (3%)
  matrix products  8.57 us (2%)
  starting transfers between devices  4.72 us (1%)
    all_gather x1, waiting for transfers between devices, per_device(): totals = jnp.sum(lax.all_gather(partial_value, 'ctg'), axis=0)  262 us
    reduce_scatter x1, waiting for transfers between devices, per_device(): lax.psum_scatter(lax.dot_general(columns, excess, (((0,), (1,)), ((), ())...  30.5 us
    all_to_all x1, waiting for transfers between devices, per_device(): lax.all_to_all(jnp.where(live_slot[None], values, 0.0).astype(jnp.bfloat1...  24.8 us
    all_to_all x1, blocking collectives, per_device(): lax.all_to_all(requests, ('ctg', 'line'), split_axis=0, concat_axis=0, ti...  20.5 us
    reduce_sum x1, other arithmetic, per_device(): totals = jnp.sum(lax.all_gather(partial_value, 'ctg'), axis=0)  16.4 us
  transfers between devices with their start and end apart: 3, of which 3 were waited for; matrix products, arithmetic and copies ran while one was open for 0% of the time, Pallas kernels for 0%

profile of v1, /device:TPU:0, one launch (start us, length us, event | category | flops | bytes accessed | tf_op | source)
XLA Modules:
  0.0 399.6 jit_solution(11246675628467044045)
XLA Ops:
  6.5 0.9 copy.22
  7.4 20.5 %all_to_all.20 = s32[128,1,15]{2,1,0:T(1,128)S(1)} all-to-all(s32[128,1,15]{2,1,0:T(1,128)S(1)} %copy.22), channel_id=1, replica_groups=mesh['ctg'=16,'line'=8] {'ctg','line'}, dimensions={0} | all-to-all | bytes 15360 | tf_op jit(solution)/shard_map/all_to_all | solution.py:14
  27.9 0.1 copy.23
  28.0 0.5 broadcast.84
  28.5 0.8 reduce.5
  29.3 0.2 all_to_all.16
  29.6 0.1 copy.24
  29.7 0.7 copy.25
  30.4 5.0 %gather_fusion = bf16[1920,384]{1,0:T(8,128)(2,1)S(1)} fusion(f32[384,120]{0,1:T(8,128)S(1)} %copy-done.1, s32[2048]{0:T(1024)S(1)} %pad_clamp_fusion), kind=kCustom, calls=%fused_computation | custom fusion | bytes 2956800 | tf_op jit(solution)/shard_map/jit(_take)/gather | solution.py:17
  35.5 0.5 gather.11
  36.0 3.1 select_convert_fusion
  39.1 4.6 %all-to-all-start.1 = ((bf16[384,128,15]{0,2,1:T(8,128)(2,1)}), bf16[384,128,15]{0,2,1:T(8,128)(2,1)S(1)}, u32[]{:S(2)}, u32[]{:S(2)}) async-start(bf16[384,128,15]{0,2,1:T(8,128)(2,1)} %select_convert_fusion), calls=%async_computation.1 | async-start | bytes 3145728 | tf_op jit(solution)/shard_map/all_to_all | solution.py:19
  43.7 0.0 all-gather.3.cloned.1.call-start
  43.8 24.8 %all-to-all-done.1 = bf16[384,128,15]{0,2,1:T(8,128)(2,1)S(1)} async-done(((bf16[384,128,15]{0,2,1:T(8,128)(2,1)}), bf16[384,128,15]{0,2,1:T(8,128)(2,1)S(1)}, u32[]{:S(2)}, u32[]{:S(2)}) %all-to-all-start.1) | async-done | bytes 1474592 | tf_op jit(solution)/shard_map/all_to_all | solution.py:19
  68.6 0.5 reshape.60
  69.1 4.1 %gather_fusion.1 = bf16[960,384]{1,0:T(8,128)(2,1)S(1)} fusion(bf16[384,1920]{0,1:T(8,128)(2,1)S(1)} %reshape.60, s32[1024]{0:T(1024)S(1)} %pad_clamp_fusion.1), kind=kCustom, calls=%fused_computation.1 | custom fusion | bytes 1478400 | tf_op jit(solution)/shard_map/jit(_take)/gather | solution.py:27
  73.2 6.7 %fusion = f32[384,1920]{1,0:T(8,128)} fusion(bf16[1920,960]{0,1:T(8,128)(2,1)} %param.8, bf16[1920,960]{0,1:T(8,128)(2,1)} %param.9, bf16[960,384]{1,0:T(8,128)(2,1)S(1)} %gather_fusion.1, pred[960]{0:T(1024)(128)(4,1)S(1)} %compare_and_fusion.1), kind=kOutput, calls=%fused_computation.3 | convolution fusion | flops 1423319040 | bytes 11060160 | tf_op jit(solution)/shard_map/dot_general | solution.py:29
  79.9 0.0 all-gather.3.cloned.1.call-update
  79.9 0.0 reduce-scatter.4.cloned.1.call-start
  80.0 262.2 %all-gather.3.cloned.1.call-done = f32[6144,1920]{1,0:T(8,128)} async-done(((f32[384,1920]{1,0:T(8,128)}), f32[6144,1920]{1,0:T(8,128)}) %all-gather.3.cloned.1.call-update) | async-done | bytes 47185936 | tf_op jit(solution)/shard_map/all_gather | solution.py:32
  342.1 16.4 %reduce_sum.9 = f32[384,1920]{1,0:T(8,128)S(1)} reduce(f32[16,384,1920]{2,1,0:T(8,128)} %bitcast.20, f32[]{:T(128)} %constant.34.clone.1), dimensions={0}, to_apply=%region_0.1 | reduce | flops 11059200 | bytes 50135044 | tf_op jit(solution)/shard_map/reduce_sum | solution.py:32
  358.6 1.9 fusion.2
  360.5 1.7 copy.27
  362.2 30.5 %reduce-scatter.4.cloned.1.call-done = f32[16,384]{1,0:T(8,128)} async-done(((f32[128,384]{1,0:T(8,128)}), f32[16,384]{1,0:T(8,128)}) %reduce-scatter.4.cloned.1.call-update) | async-done | bytes 24592 | tf_op jit(solution)/shard_map/reduce_scatter | solution.py:35
  (15 shorter events, 0.1 us)
Async XLA Ops:
  6.5 352.0 %copy-start = (bf16[1920,128]{1,0:T(8,128)(2,1)S(1)}, bf16[1920,128]{1,0:T(8,128)(2,1)}, u32[]{:S(2)}) copy-start(bf16[1920,128]{1,0:T(8,128)(2,1)} %param.11) | copy-start | bytes 1474564
  6.5 23.9 %copy-start.1 = (f32[384,120]{0,1:T(8,128)S(1)}, f32[384,120]{0,1:T(8,128)}, u32[]{:S(2)}) copy-start(f32[384,120]{0,1:T(8,128)} %param.7) | copy-start | bytes 552964
  36.0 7.8 %copy-start.2 = (s32[960]{0:T(1024)S(1)}, s32[960]{0:T(1024)}, u32[]{:S(2)}) copy-start(s32[960]{0:T(1024)} %param.13) | copy-start | bytes 11524
  39.1 29.5 %all-to-all-start.1 = ((bf16[384,128,15]{0,2,1:T(8,128)(2,1)}), bf16[384,128,15]{0,2,1:T(8,128)(2,1)S(1)}, u32[]{:S(2)}, u32[]{:S(2)}) async-start(bf16[384,128,15]{0,2,1:T(8,128)(2,1)} %select_convert_fusion), calls=%async_computation.1 | async-start | bytes 3145728 | tf_op jit(solution)/shard_map/all_to_all | solution.py:19
  43.7 298.4 %all-gather.3.cloned.1.call-start = ((), (), s32[]{:S(2)}) async-start(), calls=%async_computation.3 | async-start | bytes 50135040 | tf_op jit(solution)/shard_map/all_gather | solution.py:32
  79.9 312.8 %reduce-scatter.4.cloned.1.call-start = ((), (), s32[]{:S(2)}) async-start(), calls=%async_computation.4 | async-start | bytes 221184 | tf_op jit(solution)/shard_map/reduce_scatter | solution.py:35
  342.1 16.4 %copy-start.3 = (f32[1920]{0:T(1024)S(1)}, f32[1920]{0:T(1024)}, u32[]{:S(2)}) copy-start(f32[1920]{0:T(1024)} %param.10) | copy-start | bytes 23044
Sparse Core Ops, SparseCore 0:
  80.0 262.0 all-gather.2
  362.3 30.3 reduce-scatter.3

commit v2 on v0

--- a/solution.py
+++ b/solution.py
@@ -16,12 +16,20 @@
     columns = jnp.where(live_slot, asked, 0)
     values = jnp.take(base_flow, columns.reshape(-1), axis=1)
     values = values.reshape(columns_total, asked.shape[0], asked.shape[1])
-    replies = lax.all_to_all(
-        jnp.where(live_slot[None], values, 0.0).astype(jnp.bfloat16),
-        ("ctg", "line"),
-        split_axis=1,
-        concat_axis=1,
-        tiled=True,
+    replies = jnp.concatenate(
+        lax.all_to_all(
+            jnp.stack(
+                jnp.split(
+                    jnp.where(live_slot[None], values, 0.0).astype(jnp.bfloat16),
+                    lax.axis_size(("ctg", "line")),
+                    axis=1,
+                )
+            ),
+            ("ctg", "line"),
+            0,
+            0,
+        ),
+        axis=1,
     )
     slot_flows = replies.reshape(columns_total, -1)
     outage_flow = jnp.take(slot_flows, ctg_slot, axis=1)

time: 211 us -> 287 us (1.36)
  local copies, waits for them, and re-layouts: 13.5 us -> 90.1 us
    unnamed x9 -> x136, local copies, waits for them, and re-layouts: 0.82 us -> 76.8 us
where the time goes in v2:
time: 287 us; the launch traced here: 286 us
  waiting for transfers between devices  144 us (50%)
  local copies, waits for them, and re-layouts  90.1 us (31%)
  blocking collectives  20.5 us (7%)
  between operations  13.6 us (5%)
  matrix products  9.77 us (3%)
  starting transfers between devices  4.85 us (2%)
  other arithmetic  3.13 us (1%)
    psum x1, waiting for transfers between devices, per_device(): totals = lax.psum(partial_value, 'ctg')  89.5 us
    unnamed x136, local copies, waits for them, and re-layouts  76.8 us
    reduce_scatter x1, waiting for transfers between devices, per_device(): lax.psum_scatter(lax.dot_general(columns, excess, (((0,), (1,)), ((), ())...  30 us
    all_to_all x1, waiting for transfers between devices, per_device(): lax.all_to_all(jnp.stack(jnp.split(jnp.where(live_slot[None], values, 0.0...  24.8 us
    all_to_all x1, blocking collectives, per_device(): lax.all_to_all(requests, ('ctg', 'line'), split_axis=0, concat_axis=0, ti...  20.5 us
    dot_general x1, matrix products, per_device(): lax.dot_general(outage_flow, weighted, (((1,), (1,)), ((), ())), preferre...  6.72 us
  transfers between devices with their start and end apart: 3, of which 3 were waited for; matrix products, arithmetic and copies ran while one was open for 0% of the time, Pallas kernels for 0%

profile of v2, /device:TPU:0, one launch (start us, length us, event | category | flops | bytes accessed | tf_op | source)
XLA Modules:
  0.0 286.2 jit_solution(13972586393448621400)
XLA Ops:
  6.5 0.9 copy.22
  7.4 20.5 %all_to_all.20 = s32[128,1,15]{2,1,0:T(1,128)S(1)} all-to-all(s32[128,1,15]{2,1,0:T(1,128)S(1)} %copy.22), channel_id=1, replica_groups=mesh['ctg'=16,'line'=8] {'ctg','line'}, dimensions={0} | all-to-all | bytes 15360 | tf_op jit(solution)/shard_map/all_to_all | solution.py:14
  28.5 0.8 reduce.5
  29.7 0.7 copy.25
  30.4 5.0 %gather_fusion = bf16[1920,384]{1,0:T(8,128)(2,1)S(1)} fusion(f32[384,120]{0,1:T(8,128)S(1)} %copy-done.1, s32[2048]{0:T(1024)S(1)} %pad_clamp_fusion), kind=kCustom, calls=%fused_computation | custom fusion | bytes 2956800 | tf_op jit(solution)/shard_map/jit(_take)/gather | solution.py:17
  36.0 2.2 select_convert_fusion
  39.4 0.6 constant_dynamic-update-slice_fusion.125
  49.0 0.6 constant_dynamic-update-slice_fusion.109
  53.8 0.6 constant_dynamic-update-slice_fusion.101
  65.2 0.6 constant_dynamic-update-slice_fusion.82
  82.5 0.6 constant_dynamic-update-slice_fusion.53
  85.5 0.6 constant_dynamic-update-slice_fusion.48
  89.1 0.6 constant_dynamic-update-slice_fusion.42
  90.9 0.6 constant_dynamic-update-slice_fusion.39
  96.9 0.6 constant_dynamic-update-slice_fusion.29
  98.7 0.6 constant_dynamic-update-slice_fusion.26
  114.9 4.8 %all-to-all-start.1 = ((bf16[128,384,1,15]{1,3,2,0:T(8,128)(2,1)}), bf16[128,384,1,15]{1,3,2,0:T(8,128)(2,1)S(1)}, u32[]{:S(2)}, u32[]{:S(2)}) async-start(bf16[128,384,1,15]{1,3,2,0:T(8,128)(2,1)} %constant_dynamic-update-slice_fusion), calls=%async_computation.1 | async-start | bytes 3145728 | tf_op jit(solution)/shard_map/all_to_all | solution.py:20
  119.8 24.8 %all-to-all-done.1 = bf16[128,384,1,15]{1,3,2,0:T(8,128)(2,1)S(1)} async-done(((bf16[128,384,1,15]{1,3,2,0:T(8,128)(2,1)}), bf16[128,384,1,15]{1,3,2,0:T(8,128)(2,1)S(1)}, u32[]{:S(2)}, u32[]{:S(2)}) %all-to-all-start.1) | async-done | bytes 1474592 | tf_op jit(solution)/shard_map/all_to_all | solution.py:20
  145.1 4.1 %gather_fusion.1 = bf16[960,384]{1,0:T(8,128)(2,1)S(1)} fusion(bf16[384,1920]{0,1:T(8,128)(2,1)S(1)} %reshape_reshape.3, s32[1024]{0:T(1024)S(1)} %pad_clamp_fusion.1), kind=kCustom, calls=%fused_computation.1 | custom fusion | bytes 1478400 | tf_op jit(solution)/shard_map/jit(_take)/gather | solution.py:35
  149.2 6.7 %fusion = f32[384,1920]{1,0:T(8,128)} fusion(bf16[1920,960]{0,1:T(8,128)(2,1)} %param.8, bf16[1920,960]{0,1:T(8,128)(2,1)} %param.9, bf16[960,384]{1,0:T(8,128)(2,1)S(1)} %gather_fusion.1, pred[960]{0:T(1024)(128)(4,1)S(1)} %compare_and_fusion.1), kind=kOutput, calls=%fused_computation.3 | convolution fusion | flops 1423319040 | bytes 11060160 | tf_op jit(solution)/shard_map/dot_general | solution.py:37
  156.0 89.5 %all-reduce.2.cloned.1.call-done = f32[384,1920]{1,0:T(8,128)} async-done(((f32[384,1920]{1,0:T(8,128)}), f32[384,1920]{1,0:T(8,128)}) %all-reduce.2.cloned.1.call-update) | async-done | bytes 2949136 | tf_op jit(solution)/shard_map/psum | solution.py:40
  245.5 3.1 %fusion.2 = f32[128,384]{0,1:T(8,128)S(1)} fusion(bf16[1920,128]{1,0:T(8,128)(2,1)S(1)} %copy-done, f32[384,1920]{1,0:T(8,128)} %all-reduce.2.cloned.1.call-done, f32[1920]{0:T(1024)S(1)} %copy-done.3), kind=kOutput, calls=%fused_computation.7 | convolution fusion | flops 193167360 | bytes 3644928 | tf_op jit(solution)/shard_map/dot_general | solution.py:44
  248.5 0.8 copy.27
  249.3 30.0 %reduce-scatter.4.cloned.1.call-done = f32[16,384]{1,0:T(8,128)} async-done(((f32[128,384]{1,0:T(8,128)}), f32[16,384]{1,0:T(8,128)}) %reduce-scatter.4.cloned.1.call-update) | async-done | bytes 24592 | tf_op jit(solution)/shard_map/reduce_scatter | solution.py:43
  (142 shorter events, 72.7 us)
Async XLA Ops:
  6.5 238.9 %copy-start = (bf16[1920,128]{1,0:T(8,128)(2,1)S(1)}, bf16[1920,128]{1,0:T(8,128)(2,1)}, u32[]{:S(2)}) copy-start(bf16[1920,128]{1,0:T(8,128)(2,1)} %param.11) | copy-start | bytes 1474564
  6.5 23.9 %copy-start.1 = (f32[384,120]{0,1:T(8,128)S(1)}, f32[384,120]{0,1:T(8,128)}, u32[]{:S(2)}) copy-start(f32[384,120]{0,1:T(8,128)} %param.7) | copy-start | bytes 552964
  114.9 4.8 %copy-start.2 = (s32[960]{0:T(1024)S(1)}, s32[960]{0:T(1024)}, u32[]{:S(2)}) copy-start(s32[960]{0:T(1024)} %param.13) | copy-start | bytes 11524
  114.9 29.6 %all-to-all-start.1 = ((bf16[128,384,1,15]{1,3,2,0:T(8,128)(2,1)}), bf16[128,384,1,15]{1,3,2,0:T(8,128)(2,1)S(1)}, u32[]{:S(2)}, u32[]{:S(2)}) async-start(bf16[128,384,1,15]{1,3,2,0:T(8,128)(2,1)} %constant_dynamic-update-slice_fusion), calls=%async_computation.1 | async-start | bytes 3145728 | tf_op jit(solution)/shard_map/all_to_all | solution.py:20
  119.7 125.8 %all-reduce.2.cloned.1.call-start = ((), (), s32[]{:S(2)}) async-start(), calls=%async_computation.3 | async-start | bytes 5898240 | tf_op jit(solution)/shard_map/psum | solution.py:40
  155.9 89.6 %copy-start.3 = (f32[1920]{0:T(1024)S(1)}, f32[1920]{0:T(1024)}, u32[]{:S(2)}) copy-start(f32[1920]{0:T(1024)} %param.10) | copy-start | bytes 23044
  155.9 123.5 %reduce-scatter.4.cloned.1.call-start = ((), (), s32[]{:S(2)}) async-start(), calls=%async_computation.4 | async-start | bytes 221184 | tf_op jit(solution)/shard_map/reduce_scatter | solution.py:43
Sparse Core Ops, SparseCore 0:
  156.0 89.3 all-reduce.1
  249.5 29.8 reduce-scatter.3
